TPU v7x, 256 devices: a whole 4x4x8 slice. The times are simulated.
256 devices in a mesh: dp: 128 (over y, x, z), rep: 2 (over core).
Axes of the slice: x: 4, y: 4, z: 8, core: 2. Of those that a mesh axis runs over, the one named last changes fastest.
Arguments:
- dense_feats: bfloat16 [65536, 256], P(('dp', 'rep')), may hold values from -6 to 6
- bottom_weight: bfloat16 [256, 128], replicated, may hold values from -0.375 to 0.375
- top_weight: bfloat16 [479, 1024], replicated, may hold values from -0.25 to 0.25
- out_weight: bfloat16 [1024], replicated, may hold values from -0.1875 to 0.1875
- hot_table: bfloat16 [4096, 128], replicated, may hold values from -1.796875 to 1.796875
- cold_table: bfloat16 [524288, 128], P('dp'), may hold values from -1.796875 to 1.796875
- hot_index: int32 [65536, 13], P(('dp', 'rep')), may hold values from 0 to 4095
- cold_owner: int32 [65536, 13], P(('dp', 'rep')), may hold values from 0 to 127, all different within a row; in each aligned block of 256 rows (0 to 255, 256 to 511, ...) at most 52 rows name the same one
- cold_row: int32 [65536, 13], P(('dp', 'rep')), may hold values from 0 to 4095
- clicks: int32 [65536], P(('dp', 'rep')), may hold values from 0 to 1
Outputs:
- hot_grad: float32 [4096, 128], replicated
- cold_grad: float32 [524288, 128], P('dp')
- top_grad: float32 [479, 1024], replicated
Inputs may be any that keep to these rules, and one draw needn't show every extreme that they name: `cold_owner`: each sample names 13 different owners. Among the samples of one device no owner is named by more than 52 samples, and on some device some owner is named by exactly 52.
All inputs are finite; a program needn't handle non-finite values.
Results may differ from a plain program's by a relative error of at most 0.0061.
Values may be sent and summed in bfloat16 or wider, within the bound.
A program may use at most 64 MiB of HBM per device.

v0:
```python
import jax
import jax.numpy as jnp
import numpy as np
from jax import lax
from jax.sharding import PartitionSpec as P

FH = 13


def pair_tables(fields):
    lower_row, lower_col = np.tril_indices(fields, -1)
    picked = lower_row * fields + lower_col
    spread = np.zeros((picked.shape[0], fields * fields), np.float32)
    spread[np.arange(picked.shape[0]), picked] = 1.0
    spread[np.arange(picked.shape[0]), lower_col * fields + lower_row] = 1.0
    return (picked, spread)


def gelu_tanh(values):
    return jax.nn.gelu(values, approximate=True)


def body(
    dense_feats,
    bottom_weight,
    top_weight,
    out_weight,
    hot_table,
    cold_table,
    hot_index,
    cold_owner,
    cold_row,
    clicks,
):
    owners = lax.axis_size("dp")
    samples, cold_fields = cold_owner.shape
    width = hot_table.shape[1]
    capacity = min(samples, max(2, (2 * samples * cold_fields + owners - 1) // owners))
    fields = 1 + hot_index.shape[1] + cold_fields
    picked, spread = pair_tables(fields)
    spread_table = jnp.asarray(spread).astype(jnp.bfloat16)
    flat_owner = cold_owner.reshape(-1)
    onehot = (flat_owner[:, None] == jnp.arange(owners, dtype=jnp.int32)[None, :]).astype(jnp.int32)
    position = jnp.sum(jnp.cumsum(onehot, axis=0) * onehot, axis=1) - 1
    slot_index = flat_owner * capacity + position
    requests = jnp.zeros((owners * capacity,), jnp.int32).at[slot_index].set(cold_row.reshape(-1))
    requests = requests.reshape(owners, capacity)
    wanted = lax.all_to_all(requests, "dp", split_axis=0, concat_axis=0, tiled=True)
    found_rows = jnp.take(cold_table, wanted, axis=0)
    sent_back = lax.all_to_all(found_rows, "dp", split_axis=0, concat_axis=0, tiled=True)
    cold_vectors = jnp.take(
        sent_back.reshape(owners * capacity, width), slot_index, axis=0
    ).reshape(samples, cold_fields, width)
    hot_vectors = jnp.take(hot_table, hot_index, axis=0)
    bottom = jnp.maximum(
        jnp.dot(dense_feats, bottom_weight, preferred_element_type=jnp.float32), 0.0
    ).astype(jnp.bfloat16)
    stacked = jnp.concatenate([bottom[:, None, :], hot_vectors, cold_vectors], axis=1)
    pair_dots = jnp.einsum("bie,bje->bij", stacked, stacked, preferred_element_type=jnp.float32)
    lower_pairs = pair_dots.reshape(samples, fields * fields)[:, picked].astype(jnp.bfloat16)
    interact = jnp.concatenate([bottom, lower_pairs], axis=1)
    hidden_pre = jnp.dot(interact, top_weight, preferred_element_type=jnp.float32)
    activated, act_back = jax.vjp(gelu_tanh, hidden_pre)
    hidden = activated.astype(jnp.bfloat16)
    logits = jnp.dot(hidden, out_weight, preferred_element_type=jnp.float32)
    errors = jax.nn.sigmoid(logits) - clicks.astype(jnp.float32)
    (grad_pre,) = act_back(errors[:, None] * out_weight.astype(jnp.float32)[None, :])
    grad_pre = grad_pre.astype(jnp.bfloat16)
    top_term = lax.dot_general(
        interact, grad_pre, (((0,), (0,)), ((), ())), preferred_element_type=jnp.float32
    )
    grad_inter = lax.dot_general(
        grad_pre, top_weight, (((1,), (1,)), ((), ())), preferred_element_type=jnp.float32
    )
    grad_pairs = grad_inter[:, width:].astype(jnp.bfloat16)
    symmetric = jnp.dot(grad_pairs, spread_table, preferred_element_type=jnp.float32).reshape(
        samples, fields, fields
    )
    grad_stack = jnp.einsum(
        "bij,bje->bie", symmetric.astype(jnp.bfloat16), stacked, preferred_element_type=jnp.float32
    )
    cold_terms = grad_stack[:, 1 + FH :].astype(jnp.bfloat16).reshape(samples * cold_fields, width)
    outgoing = jnp.zeros((owners * capacity, width), jnp.bfloat16).at[slot_index].set(cold_terms)
    returned = lax.all_to_all(
        outgoing.reshape(owners, capacity, width), "dp", split_axis=0, concat_axis=0, tiled=True
    )
    local_cold = (
        jnp.zeros((cold_table.shape[0], width), jnp.float32)
        .at[wanted.reshape(-1)]
        .add(returned.reshape(owners * capacity, width).astype(jnp.float32))
    )
    cold_grad = lax.psum(local_cold, "rep")
    local_hot = (
        jnp.zeros(hot_table.shape, jnp.float32)
        .at[hot_index.reshape(-1)]
        .add(grad_stack[:, 1 : 1 + FH].reshape(-1, width))
    )
    top_grad = lax.psum(top_term, ("dp", "rep"))
    hot_grad = lax.psum(local_hot, ("dp", "rep"))
    return (hot_grad, cold_grad, top_grad)


def solution(mesh):
    return jax.shard_map(
        body,
        mesh=mesh,
        in_specs=(
            P(("dp", "rep"), None),
            P(),
            P(),
            P(),
            P(),
            P("dp", None),
            P(("dp", "rep"), None),
            P(("dp", "rep"), None),
            P(("dp", "rep"), None),
            P(("dp", "rep")),
        ),
        out_specs=(P(), P("dp", None), P()),
        check_vma=False,
    )
```

profile of v0, /device:TPU:1, one launch (start us, length us, event | category | flops | bytes accessed | tf_op | source)
XLA Modules:
  0.0 531.7 jit_solution(13914842688294364258)
XLA Ops:
  11.2 2.0 fusion.2
  14.0 12.8 %scatter_custom_fusion = s32[6656]{0:T(1024)S(1)} fusion(s32[3328]{0:T(1024)S(1)} %fusion.30, s32[3328]{0:T(1024)S(1)} %reshape.253, s32[]{:T(128)} %constant.28.clone.1), kind=kCustom, calls=%fused_computation.68 | custom fusion | bytes 26628 | tf_op jit(solution)/shard_map/scatter | solution.py:46
  26.9 26.7 %all_to_all.25 = s32[128,1,52]{2,1,0:T(1,128)S(1)} all-to-all(s32[128,1,52]{2,1,0:T(1,128)S(1)} %bitcast.35), channel_id=1, replica_groups=mesh['dp'=128,'rep'=2] {'dp'}, dimensions={0} | all-to-all | bytes 53248 | tf_op jit(solution)/shard_map/all_to_all | solution.py:48
  53.8 12.5 %gather_fusion.1 = bf16[6656,128]{1,0:T(8,128)(2,1)S(1)} fusion(bf16[4096,128]{1,0:T(8,128)(2,1)S(1)} %copy-done, s32[7168]{0:T(1024)S(1)} %pad_clamp_fusion), kind=kCustom, calls=%fused_computation.1 | custom fusion | bytes 3434496 | tf_op jit(solution)/shard_map/jit(_take)/gather | solution.py:49
  67.7 4.2 broadcast_select_fusion
  71.9 7.6 %all-to-all-start.1 = ((bf16[128,52,128]{2,1,0:T(8,128)(2,1)}), bf16[128,52,128]{2,1,0:T(8,128)(2,1)}, u32[]{:S(2)}, u32[]{:S(2)}) async-start(bf16[128,52,128]{2,1,0:T(8,128)(2,1)} %broadcast_select_fusion), calls=%async_computation.1 | async-start | bytes 3670016 | tf_op jit(solution)/shard_map/all_to_all | solution.py:50
  80.4 6.5 %gather_fusion = bf16[3328,128]{1,0:T(8,128)(2,1)S(1)} fusion(bf16[4096,128]{1,0:T(8,128)(2,1)S(1)} %copy-done.2, s32[4096]{0:T(1024)S(1)} %pad_clamp_fusion.2), kind=kCustom, calls=%fused_computation | custom fusion | bytes 1717248 | tf_op jit(solution)/shard_map/jit(_take)/gather | solution.py:54
  87.8 36.9 %all-to-all-done.1 = bf16[128,52,128]{2,1,0:T(8,128)(2,1)} async-done(((bf16[128,52,128]{2,1,0:T(8,128)(2,1)}), bf16[128,52,128]{2,1,0:T(8,128)(2,1)}, u32[]{:S(2)}, u32[]{:S(2)}) %all-to-all-start.1) | async-done | bytes 1703968 | tf_op jit(solution)/shard_map/all_to_all | solution.py:50
  124.7 2.4 reshape.210
  127.1 7.7 %gather_fusion.2 = bf16[3328,128]{1,0:T(8,128)(2,1)} fusion(bf16[6656,128]{1,0:T(8,128)(2,1)S(1)} %reshape.210, s32[4096]{0:T(1024)S(1)} %pad_clamp_fusion.1), kind=kCustom, calls=%fused_computation.2 | custom fusion | bytes 1717248 | tf_op jit(solution)/shard_map/jit(_take)/gather | solution.py:51
  138.9 2.4 fusion.22
  141.2 4.2 reshape.286
  150.4 3.2 copy.66
  153.6 2.5 fusion.21
  159.5 14.5 %scatter_custom_fusion.2 = bf16[6656,128]{1,0:T(8,128)(2,1)S(1)} fusion(s32[3328]{0:T(1024)S(1)} %fusion.30, bf16[3328,128]{1,0:T(8,128)(2,1)} %reshape.269, bf16[]{:T(256)} %constant.82.clone.1), kind=kCustom, calls=%fused_computation.43 | custom fusion | bytes 1704448 | tf_op jit(solution)/shard_map/scatter | solution.py:83
  175.4 7.3 %all-to-all-start.2 = ((bf16[128,52,128]{2,1,0:T(8,128)(2,1)}), bf16[128,52,128]{2,1,0:T(8,128)(2,1)}, u32[]{:S(2)}, u32[]{:S(2)}) async-start(bf16[128,52,128]{2,1,0:T(8,128)(2,1)} %reshape.215), calls=%async_computation.2 | async-start | bytes 3670016 | tf_op jit(solution)/shard_map/all_to_all | solution.py:84
  183.1 2.1 slice.33
  186.6 21.4 %scatter_custom_fusion.1 = f32[4096,128]{1,0:T(8,128)} fusion(s32[3328]{0:T(1024)S(1)} %fusion.29, f32[3328,128]{1,0:T(8,128)} %reshape.261, f32[]{:T(128)} %constant.27.clone.1), kind=kCustom, calls=%fused_computation.39 | custom fusion | flops 425984 | bytes 2097664 | tf_op jit(solution)/shard_map/scatter-add | solution.py:96
  211.5 14.6 %all-to-all-done.2 = bf16[128,52,128]{2,1,0:T(8,128)(2,1)} async-done(((bf16[128,52,128]{2,1,0:T(8,128)(2,1)}), bf16[128,52,128]{2,1,0:T(8,128)(2,1)}, u32[]{:S(2)}, u32[]{:S(2)}) %all-to-all-start.2) | async-done | bytes 1703968 | tf_op jit(solution)/shard_map/all_to_all | solution.py:84
  226.1 3.9 reshape.277
  229.9 37.6 %scatter_custom_fusion.3 = f32[4096,128]{1,0:T(8,128)} fusion(s32[6656]{0:T(1024)S(1)} %fusion.26, f32[6656,128]{1,0:T(8,128)} %reshape.277, f32[]{:T(128)} %constant.27.clone.1), kind=kCustom, calls=%fused_computation.37 | custom fusion | flops 851968 | bytes 2097664 | tf_op jit(solution)/shard_map/scatter-add | solution.py:90
  267.6 214.1 %all-reduce.6.cloned.1.call-done = (f32[4096,128]{1,0:T(8,128)}, f32[479,1024]{1,0:T(8,128)}) async-done(((f32[4096,128]{1,0:T(8,128)}, f32[479,1024]{1,0:T(8,128)}), (f32[4096,128]{1,0:T(8,128)}, f32[479,1024]{1,0:T(8,128)})) %all-reduce.6.cloned.1.call-update) | async-done | bytes 4059152 | tf_op jit(solution)/shard_map/psum | solution.py:99
  481.6 36.4 %all-reduce.4.cloned.1.call-done = f32[4096,128]{1,0:T(8,128)} async-done(((f32[4096,128]{1,0:T(8,128)}), f32[4096,128]{1,0:T(8,128)}) %all-reduce.4.cloned.1.call-update) | async-done | bytes 2097168 | tf_op jit(solution)/shard_map/psum | solution.py:92
  518.1 3.2 copy.71
  (106 shorter events, 30.4 us)
Async XLA Ops:
  7.2 46.6 %copy-start = (bf16[4096,128]{1,0:T(8,128)(2,1)S(1)}, bf16[4096,128]{1,0:T(8,128)(2,1)}, u32[]{:S(2)}) copy-start(bf16[4096,128]{1,0:T(8,128)(2,1)} %param.18) | copy-start | bytes 3145732
  10.2 3.4 copy-start.15
  71.9 7.8 %copy-start.16 = (bf16[1024]{0:T(1024)(128)(2,1)S(1)}, bf16[1024]{0:T(1024)(128)(2,1)}, u32[]{:S(2)}) copy-start(bf16[1024]{0:T(1024)(128)(2,1)} %param.16) | copy-start | bytes 6148
  71.9 7.9 %copy-start.11 = (s32[256,13]{0,1:T(8,128)S(1)}, s32[256,13]{0,1:T(8,128)}, u32[]{:S(2)}) copy-start(s32[256,13]{0,1:T(8,128)} %param.20) | copy-start | bytes 39940
  71.9 8.1 %copy-start.12 = (s32[256,13]{0,1:T(8,128)S(1)}, s32[256,13]{0,1:T(8,128)}, u32[]{:S(2)}) copy-start(s32[256,13]{0,1:T(8,128)} %param.19) | copy-start | bytes 39940
  71.9 8.5 %copy-start.2 = (bf16[4096,128]{1,0:T(8,128)(2,1)S(1)}, bf16[4096,128]{1,0:T(8,128)(2,1)}, u32[]{:S(2)}) copy-start(bf16[4096,128]{1,0:T(8,128)(2,1)} %param.17) | copy-start | bytes 3145732
  71.9 52.8 %all-to-all-start.1 = ((bf16[128,52,128]{2,1,0:T(8,128)(2,1)}), bf16[128,52,128]{2,1,0:T(8,128)(2,1)}, u32[]{:S(2)}, u32[]{:S(2)}) async-start(bf16[128,52,128]{2,1,0:T(8,128)(2,1)} %broadcast_select_fusion), calls=%async_computation.1 | async-start | bytes 3670016 | tf_op jit(solution)/shard_map/all_to_all | solution.py:50
  80.4 7.0 %copy-start.13 = (bf16[256,256]{1,0:T(8,128)(2,1)S(1)}, bf16[256,256]{1,0:T(8,128)(2,1)}, u32[]{:S(2)}) copy-start(bf16[256,256]{1,0:T(8,128)(2,1)} %param.13) | copy-start | bytes 393220
  80.4 7.0 %copy-start.14 = (bf16[256,128]{1,0:T(8,128)(2,1)S(1)}, bf16[256,128]{1,0:T(8,128)(2,1)}, u32[]{:S(2)}) copy-start(bf16[256,128]{1,0:T(8,128)(2,1)} %param.14) | copy-start | bytes 196612
  87.0 0.8 copy-start.17
  87.8 49.8 %copy-start.10 = (bf16[256,1,128]{2,1,0:T(2,128)(2,1)}, bf16[256,1,128]{2,1,0:T(2,128)(2,1)S(1)}, u32[]{:S(2)}) copy-start(bf16[256,1,128]{2,1,0:T(2,128)(2,1)S(1)} %copy.64) | copy-start | bytes 196612
  137.6 1.0 copy-start.4
  137.6 1.3 copy-start.5
  141.2 6.4 %copy-start.6 = (bf16[479,1024]{1,0:T(8,128)(2,1)S(1)}, bf16[479,1024]{1,0:T(8,128)(2,1)}, u32[]{:S(2)}) copy-start(bf16[479,1024]{1,0:T(8,128)(2,1)} %param.15) | copy-start | bytes 2942980
  147.7 0.9 copy-start.18
  148.6 1.3 copy-start.9
  156.1 1.9 copy-start.3
  175.4 50.6 %all-to-all-start.2 = ((bf16[128,52,128]{2,1,0:T(8,128)(2,1)}), bf16[128,52,128]{2,1,0:T(8,128)(2,1)}, u32[]{:S(2)}, u32[]{:S(2)}) async-start(bf16[128,52,128]{2,1,0:T(8,128)(2,1)} %reshape.215), calls=%async_computation.2 | async-start | bytes 3670016 | tf_op jit(solution)/shard_map/all_to_all | solution.py:84
  182.7 298.9 %all-reduce.6.cloned.1.call-start = ((), (), s32[]{:S(2)}) async-start(), calls=%async_computation.4 | async-start | bytes 8126464 | tf_op jit(solution)/shard_map/psum | solution.py:99
  209.7 308.3 %all-reduce.4.cloned.1.call-start = ((), (), s32[]{:S(2)}) async-start(), calls=%async_computation.3 | async-start | bytes 4194304 | tf_op jit(solution)/shard_map/psum | solution.py:92
  518.1 3.2 copy-start.7
  521.3 2.3 copy-start.8
  521.3 3.6 copy-start.1
Sparse Core Ops, SparseCore 0:
  209.9 271.7 all-reduce.5
  485.0 33.0 all-reduce.3
where the time goes:
time: 532 us
  waiting for transfers between devices  302 us (57%)
  local copies, waits for them, and re-layouts  94.7 us (18%)
  other arithmetic  70.2 us (13%)
  blocking collectives  26.7 us (5%)
  starting transfers between devices  14.9 us (3%)
  between operations  14.6 us (3%)
  matrix products  8.56 us (2%)
    psum x1, waiting for transfers between devices, body(): hot_grad = lax.psum(local_hot, ('dp', 'rep'))  214 us
    scatter-add x1, other arithmetic, body(): local_cold = jnp.zeros((cold_table.shape[0], width), jnp.float32).at[want...  37.6 us
    all_to_all x1, waiting for transfers between devices, body(): lax.all_to_all(found_rows, 'dp', split_axis=0, concat_axis=0, tiled=True)  36.9 us
    psum x1, waiting for transfers between devices, body(): cold_grad = lax.psum(local_cold, 'rep')  36.4 us
    all_to_all x1, blocking collectives, body(): lax.all_to_all(requests, 'dp', split_axis=0, concat_axis=0, tiled=True)  26.7 us
    scatter-add x1, other arithmetic, body(): local_hot = jnp.zeros(hot_table.shape, jnp.float32).at[hot_index.reshape(...  21.4 us
    all_to_all x1, waiting for transfers between devices, body(): lax.all_to_all(outgoing.reshape(owners, capacity, width), 'dp', split_axi...  14.6 us
    scatter x1, local copies, waits for them, and re-layouts, body(): jnp.zeros((owners * capacity, width), jnp.bfloat16).at[slot_index]  14.5 us
  transfers between devices with their start and end apart: 4, of which 4 were waited for; matrix products, arithmetic and copies ran while one was open for 15% of the time, Pallas kernels for 0%

commit v1 on v0

v1 whole, which is shorter than its diff:
```python
import jax
import jax.numpy as jnp
from jax import lax
from jax.experimental import pallas as pl
from jax.experimental.pallas import tpu as pltpu
from jax.sharding import PartitionSpec as P

MESH = pl.DeviceIdType.MESH
NX, NY, NZ = 4, 4, 8
VMEM_LIMIT = 60 * 1024 * 1024
F32 = jnp.float32
BF16 = jnp.bfloat16
CAP = 52
EARLY = 48
UNROLL = 4


def place():
    me = lax.axis_index("dp")
    core = lax.axis_index("rep")
    z = lax.rem(me, NZ)
    x = lax.rem(lax.div(me, NZ), NX)
    y = lax.div(me, NZ * NX)
    return x, y, z, core


def peer(x, y, z, core):
    return (y * (NX * NZ) + x * NZ + z, core)


def rows_at(start, size):
    return pl.ds(pl.multiple_of(start, 16), size)


def params():
    return pltpu.CompilerParams(vmem_limit_bytes=VMEM_LIMIT)


def iota(shape, dimension):
    return lax.broadcasted_iota(jnp.int32, shape, dimension)


def build_tables(x, y, z, owner_ref, row_ref, query_ref, term_ref, place_ref, rank, rows, table):
    fill = jnp.zeros((115, 256), F32)
    owner = jnp.concatenate([owner_ref[...].astype(F32), fill], axis=0).T.astype(jnp.int32)
    row = jnp.concatenate([row_ref[...].astype(F32), fill], axis=0).T
    dz = (lax.bitwise_and(owner, 7) - z + 8) & 7
    dx = (lax.bitwise_and(lax.shift_right_logical(owner, 3), 3) - x + 4) & 3
    dy = (lax.shift_right_logical(owner, 5) - y + 4) & 3
    relative = dz * 16 + dy * 4 + dx
    lane = iota((256, 128), 1)
    named = jnp.zeros((256, 128), F32)
    wanted = jnp.zeros((256, 128), F32)
    number = jnp.zeros((256, 128), F32)
    sample = (iota((256, 128), 0) + 8).astype(F32)
    for f in range(13):
        here = relative[:, f : f + 1] == lane
        named = jnp.where(here, 1.0, named)
        wanted = jnp.where(here, row[:, f : f + 1], wanted)
        number = jnp.where(here, sample + float(f * 256), number)
    before = jnp.where(iota((256, 256), 1) < iota((256, 256), 0), 1.0, 0.0).astype(BF16)
    count = jnp.dot(before, named.astype(BF16), preferred_element_type=F32)
    back_x = (4 - dx) & 3
    block = ((((4 - dy) & 3) * 4 + back_x) * 8 + ((8 - dz) & 7)) * 64
    block, late = block.astype(F32), (4 * back_x).astype(F32)
    places = jnp.zeros((256, 128), F32)
    for f in range(13):
        here = relative[:, f : f + 1] == lane
        mine = jnp.minimum(jnp.sum(jnp.where(here, count, 0.0), axis=1, keepdims=True), float(CAP - 1))
        inside = jnp.where(mine < float(EARLY), mine, mine + late[:, f : f + 1])
        places = jnp.where(lane == f, block[:, f : f + 1] + inside, places)
    place_ref[...] = jnp.clip(places.T[0:16, :].astype(jnp.int32), 0, 8191)
    rank[...] = jnp.where(named > 0.0, count, -1.0)
    rows[...] = wanted
    table[...] = jnp.zeros((128, 128), F32)

    for p in range(CAP):
        chosen = jnp.sum(jnp.where(rank[...] == float(p), rows[...], 0.0), axis=0, keepdims=True)
        if p < EARLY:
            table[p : p + 1, :] = chosen
        else:
            for e in range(4):
                at = EARLY + e * 4 + p - EARLY
                table[at : at + 1, :] = jnp.where((iota((1, 128), 1) & 3) == e, chosen, -1.0)

    query_ref[...] = table[...].T.astype(jnp.int32).reshape(8, 16, 128)
    rows[...] = number
    for p in range(CAP):
        table[p : p + 1, :] = jnp.sum(jnp.where(rank[...] == float(p), rows[...], 0.0), axis=0, keepdims=True)
    term_ref[...] = jnp.clip(table[...].T.astype(jnp.int32), 0, 3335).reshape(8, 16, 128)


def widen(wide, ref, rows):
    @pl.loop(0, rows // 256)
    def _(step):
        here = pl.ds(pl.multiple_of(step * 256, 256), 256)
        wide[here, :] = ref[here, :].astype(F32)


def main_kernel(
    place_ref, got_ref, near_ref, bottom_ref, weight0_ref, weight_ref, out_weight_ref, click_ref,
    hot_ref, low_ref, grad_ref, terms,
    wide, stack, far, pairs, hidden, slope,
):
    for k in range(16):
        for d in range(8):
            at = (k * 8 + d) * 64
            wide[at : at + 64, :] = got_ref[k, d].astype(F32)
    for e in range(UNROLL):
        far[e, 104:144, :] = jnp.zeros((40, 128), F32)
    same = (iota((256, 256), 0) & 7) == (iota((256, 256), 1) & 7)
    fold = jnp.where((iota((256, 128), 0) >> 3) == (iota((256, 128), 1) & 31), 1.0, 0.0).astype(BF16)
    unfold = jnp.where((iota((128, 256), 1) >> 3) == (iota((128, 256), 0) & 31), 1.0, 0.0).astype(BF16)
    quarter = iota((8, 128), 1) >> 5
    zero8 = jnp.zeros((8, 128), F32)

    @pl.loop(0, 32 // UNROLL)
    def _(step):
        groups = [step * UNROLL + e for e in range(UNROLL)]
        for e, g in enumerate(groups):
            for f in range(13):
                for k in range(8):
                    far[e, f * 8 + k : f * 8 + k + 1, :] = wide[pl.ds(place_ref[f, g * 8 + k], 1), :]
        values = [jnp.concatenate([near_ref[g], far[e].astype(BF16)], axis=0) for e, g in enumerate(groups)]
        dots = [
            lax.dot_general(value, value, (((1,), (1,)), ((), ())), preferred_element_type=F32) for value in values
        ]
        dots = [jnp.where(same, dot, 0.0).astype(BF16) for dot in dots]
        folds = [jnp.dot(dot, fold, preferred_element_type=F32) for dot in dots]
        for e, g in enumerate(groups):
            stack[g] = values[e]
            for b in range(7):
                block = zero8
                for q in range(4):
                    i = 4 * b + q
                    block = jnp.where(quarter == q, folds[e][i * 8 : i * 8 + 8, :], block)
                pairs[pl.ds(pl.multiple_of(g * 8, 8), 8), b * 128 : b * 128 + 128] = block

    for b in range(7):
        i = 4 * b + (iota((256, 128), 1) >> 5)
        j = iota((256, 128), 1) & 31
        low_ref[:, b * 128 : b * 128 + 128] = jnp.where(i > j, pairs[:, b * 128 : b * 128 + 128], 0.0).astype(BF16)

    total = jnp.zeros((256, 128), F32)
    for n in range(4):
        here = slice(n * 256, n * 256 + 256)
        hidden[:, here] = jnp.dot(bottom_ref[...], weight0_ref[0:128, here], preferred_element_type=F32) + jnp.dot(
            low_ref[...], weight_ref[:, here], preferred_element_type=F32
        )
    for n in range(8):
        here = slice(n * 128, n * 128 + 128)
        v = hidden[:, here]
        c = 0.7978845608028654
        square = v * v
        t = jnp.tanh(c * v * (1.0 + 0.044715 * square))
        weight = out_weight_ref[:, here].astype(F32)
        act = (0.5 * v * (1.0 + t)).astype(BF16).astype(F32)
        total = total + act * weight
        slope[:, here] = weight * (0.5 * (1.0 + t) + 0.5 * c * v * (1.0 - t * t) * (1.0 + 0.134145 * square))
    logits = jnp.sum(total, axis=1, keepdims=True)
    clicks = jnp.broadcast_to(click_ref[...].astype(F32), (128, 256)).T[:, 0:1]
    errors = 1.0 / (1.0 + jnp.exp(-logits)) - clicks
    grad_ref[...] = (slope[...] * errors).astype(BF16)
    for b in range(7):
        here = slice(b * 128, b * 128 + 128)
        pairs[:, here] = lax.dot_general(
            grad_ref[...], weight_ref[here, :], (((1,), (1,)), ((), ())), preferred_element_type=F32
        )

    terms[0:8, :] = zero8

    @pl.loop(0, 32 // UNROLL)
    def _(step):
        groups = [step * UNROLL + e for e in range(UNROLL)]
        spreads = []
        for g in groups:
            rows = []
            for b in range(7):
                block = pairs[pl.ds(pl.multiple_of(g * 8, 8), 8), b * 128 : b * 128 + 128]
                for q in range(4):
                    rows.append(jnp.where(quarter == q, block, 0.0))
            rows += [zero8] * 4
            spreads.append(jnp.concatenate(rows, axis=0).astype(BF16))
        spreads = [jnp.dot(spread, unfold, preferred_element_type=F32) for spread in spreads]
        spreads = [jnp.where(same, spread, 0.0).astype(BF16) for spread in spreads]
        results = [jnp.dot(spread, stack[g], preferred_element_type=F32) for spread, g in zip(spreads, groups)]
        for e, g in enumerate(groups):
            for f in range(13):
                hot_ref[f, pl.ds(pl.multiple_of(g * 8, 8), 8), :] = results[e][8 + f * 8 : 16 + f * 8, :]
                terms[pl.ds(pl.multiple_of(8 + f * 256 + g * 8, 8), 8), :] = results[e][112 + f * 8 : 120 + f * 8, :]


def hot_kernel(row_ref, value_ref, bottom_ref, low_ref, grad_ref, out_ref, halves, top):
    columns = jnp.concatenate([(row_ref[...] >> 11).astype(F32), jnp.zeros((115, 256), F32)], axis=0).T
    for f in range(13):
        high = columns[:, f : f + 1]
        value = value_ref[f]
        halves[f * 256 : f * 256 + 256, 0:128] = jnp.where(high == 0.0, value, 0.0).astype(BF16)
        halves[f * 256 : f * 256 + 256, 128:256] = jnp.where(high == 0.0, 0.0, value).astype(BF16)

    @pl.loop(0, 8)
    def _(m):
        start = pl.multiple_of(m * 256, 256)
        wanted = iota((256, 256), 0) + m * 256
        hits = [
            jnp.where((jnp.broadcast_to(row_ref[f : f + 1, :], (256, 256)) & 2047) == wanted, 1.0, 0.0).astype(BF16)
            for f in range(13)
        ]
        total = jnp.dot(jnp.concatenate(hits, axis=1), halves[...], preferred_element_type=F32)
        out_ref[pl.ds(start, 256), :] = total[:, 0:128].astype(BF16)
        out_ref[pl.ds(start + 2048, 256), :] = total[:, 128:256].astype(BF16)

    top[472:480, :] = jnp.zeros((8, 1024), F32)
    top[0:128, :] = lax.dot_general(
        bottom_ref[...], grad_ref[...], (((0,), (0,)), ((), ())), preferred_element_type=F32
    )
    for b in range(7):
        part = lax.dot_general(
            low_ref[:, b * 128 : b * 128 + 128], grad_ref[...], (((0,), (0,)), ((), ())), preferred_element_type=F32
        )
        for q in range(4):
            i = 4 * b + q
            if 0 < i < 27:
                at = 128 + i * (i - 1) // 2
                top[at : at + i, :] = part[q * 32 : q * 32 + i, :]
    for n in range(8):
        out_ref[4096 + n * 480 : 4576 + n * 480, :] = top[:, n * 128 : n * 128 + 128].astype(BF16)
    out_ref[7936:8192, :] = jnp.zeros((256, 128), BF16)


def cold_start(want_ref, got, halves, joined):
    even, odd = want_ref[pl.ds(0, 64, stride=2), :], want_ref[pl.ds(1, 64, stride=2), :]
    both = jnp.where(iota((64, 128), 1) < 64, even, pltpu.roll(odd, 64, 1))
    joined[...] = jnp.where(both < 0, -1, both & 2047)
    columns = (want_ref[...] >> 11).astype(F32).T
    for r in range(128):
        high = columns[0:64, r : r + 1]
        value = got[r // 8, r % 8].astype(F32)
        halves[r * 64 : r * 64 + 64, 0:128] = jnp.where(high == 0.0, value, 0.0).astype(BF16)
        halves[r * 64 : r * 64 + 64, 128:256] = jnp.where(high == 0.0, 0.0, value).astype(BF16)


def cold_step(part, out_ref, halves, joined):
    @pl.loop(part * 2, part * 2 + 2)
    def _(m):
        start = pl.multiple_of(m * 256, 256)
        wanted = iota((256, 128), 0) + m * 256
        total = jnp.zeros((256, 256), F32)
        for n in range(4):
            hits = [
                jnp.where(jnp.broadcast_to(joined[t : t + 1, :], (256, 128)) == wanted, 1.0, 0.0).astype(BF16)
                for t in range(n * 16, n * 16 + 16)
            ]
            total = total + jnp.dot(
                jnp.concatenate(hits, axis=1), halves[n * 2048 : n * 2048 + 2048, :], preferred_element_type=F32
            )
        out_ref[pl.ds(start, 256), :] = total[:, 0:128].astype(BF16)
        out_ref[pl.ds(start + 2048, 256), :] = total[:, 128:256].astype(BF16)


def whole_kernel(
    owner_far, row_far, table_far, index_far, hot_table_far, dense_far, weight_far, top_far, out_weight_ref,
    click_ref,
    out_ref, part_ref, other_ref,
    owner_ref, row_ref, table_ref, hot_row_ref, hot_table_ref, dense_ref, weight_ref, top_ref, tall, query_ref,
    term_turn, place_turn, rank, rows, table, want_ref, want_flat, middle, turned, safe, wide, wide_hot, held, chosen,
    passing, got_ref, near_ref, bottom_ref, square_ref, hot_value_ref, low_ref, grad_ref, terms, rows_in, stack,
    far, pairs, hidden, slope, in_ref, hot_halves, top, leaving, onward, come, halves, joined, core_buf, half,
    buf1, sum1, buf2, sum2, buf3, index_ref, wanted, term_at, place_at,
    send_sem, recv_sem, local_sem,
):
    x, y, z, core = place()
    plane = [(dx, dy) for dy in range(4) for dx in range(4)]
    partner = peer(x, y, z, 1 - core)
    zs = [peer(x, y, lax.rem(z + d, NZ), core) for d in range(1, NZ)]
    xys = [peer(lax.rem(x + dx, NX), lax.rem(y + dy, NY), z, core) for dx, dy in plane[1:]]
    xs = [xys[d - 1] for d in range(1, 4)]
    ys = [xys[4 * d - 1] for d in range(1, 4)]
    barrier = pltpu.get_barrier_semaphore()
    everyone = [partner] + zs + xys
    for device in everyone:
        pl.semaphore_signal(barrier, inc=1, device_id=device, device_id_type=MESH)
    fetched = (
        (owner_far, owner_ref), (row_far, row_ref), (table_far, table_ref), (index_far, index_ref),
        (index_far, hot_row_ref), (hot_table_far, hot_table_ref), (dense_far, dense_ref),
        (weight_far, weight_ref), (top_far, top_ref),
    )
    fetches = [pltpu.make_async_copy(src, dst, local_sem.at[3 + n]) for n, (src, dst) in enumerate(fetched)]
    for fetch in fetches:
        fetch.start()
    fetches[0].wait()
    fetches[1].wait()
    build_tables(x, y, z, owner_ref, row_ref, query_ref, term_turn, place_turn, rank, rows, table)
    staged = [
        pltpu.make_async_copy(term_turn, term_at, local_sem.at[1]),
        pltpu.make_async_copy(place_turn, place_at, local_sem.at[2]),
    ]
    for copy in staged:
        copy.start()
    pl.semaphore_wait(barrier, len(everyone))

    started = []

    def send(src, dst, device):
        index = len(started)
        copy = pltpu.make_async_remote_copy(
            src_ref=src, dst_ref=dst, send_sem=send_sem.at[index], recv_sem=recv_sem.at[index],
            device_id=device, device_id_type=MESH,
        )
        copy.start()
        started.append(copy)
        return copy

    copies = [send(query_ref.at[d], middle.at[d], zs[d - 1]) for d in range(1, 8)]
    middle[0] = query_ref[0]
    fetches[2].wait()
    widen(wide, table_ref, 4096)
    for copy in copies:
        copy.wait_recv()
    for d in range(8):
        for k in range(16):
            turned[k, d : d + 1, :] = middle[d, k : k + 1, :]
    copies = [send(turned.at[k], want_ref.at[k], xys[k - 1]) for k in range(1, 16)]
    want_ref[0] = turned[0]
    for copy in copies:
        copy.wait_recv()
    for k in range(16):
        safe[k] = jnp.clip(want_ref[k], 0, 4095)
    copy = pltpu.make_async_copy(safe, wanted, local_sem.at[0])
    copy.start()
    copy.wait()

    order = (2, 1, 3, 0)
    along = {}
    copies = []

    def collect(dy):
        @pl.loop(0, 8)
        def _(d):
            back = lax.rem(8 - d, 8)
            for tile in range(13):
                rows = []
                for e in range(16):
                    dx, p = (tile // 3, tile % 3 * 16 + e) if tile < 12 else (e // 4, EARLY + (4 - e // 4) % 4 * 4 + e % 4)
                    k = (4 - dy) % 4 * 4 + (4 - dx) % 4
                    rows.append(wide[pl.ds(wanted[k, back, p], 1), :])
                chosen[dy, d, tile * 16 : tile * 16 + 16, :] = jnp.concatenate(rows, axis=0).astype(BF16)

        for d in range(1, 8):
            along[dy, d] = send(chosen.at[dy, d], passing.at[dy, d], zs[d - 1])
        passing[dy, 0] = chosen[dy, 0]

    def pass_on(dy):
        for d in range(1, 8):
            along[dy, d].wait_recv()
        for dx in range(4):
            early = passing.at[dy, :, pl.ds(dx * EARLY, EARLY)]
            late = passing.at[dy, :, pl.ds(4 * EARLY, 16)]
            k = dy * 4 + dx
            if k:
                copies.append(send(early, got_ref.at[k, :, pl.ds(0, EARLY)], xys[k - 1]))
                copies.append(send(late, got_ref.at[k, :, pl.ds(EARLY, 16)], xys[k - 1]))
            else:
                got_ref[0, :, 0:EARLY, :] = passing[0, :, 0:EARLY, :]
                got_ref[0, :, EARLY:64, :] = passing[0, :, 4 * EARLY : 4 * EARLY + 16, :]

    for dy in order:
        collect(dy)
    for fetch in fetches[3:]:
        fetch.wait()
    widen(wide_hot, hot_table_ref, 4096)
    bottom = jnp.maximum(jnp.dot(dense_ref[...], weight_ref[...], preferred_element_type=F32), 0.0)
    bottom_ref[...] = bottom.astype(BF16)
    held[...] = bottom

    @pl.loop(0, 32)
    def _(g):
        near_ref[g, 0:16, :] = jnp.concatenate(
            [held[pl.ds(pl.multiple_of(g * 8, 8), 8), :]]
            + [wide_hot[pl.ds(index_ref[0, g * 8 + k], 1), :] for k in range(8)], axis=0
        ).astype(BF16)
        for f in range(1, 13, 2):
            rows = [wide_hot[pl.ds(index_ref[f + k // 8, g * 8 + k % 8], 1), :] for k in range(16)]
            near_ref[g, 8 + f * 8 : 24 + f * 8, :] = jnp.concatenate(rows, axis=0).astype(BF16)

    pass_on(order[0])
    pass_on(order[1])
    tall[464:512, :] = jnp.zeros((48, 1024), BF16)
    tall[0:479, :] = top_ref[...]

    @pl.loop(0, 7)
    def _(b):
        i = 4 * b + (iota((128, 512), 0) >> 5)
        j = iota((128, 512), 0) & 31
        high, low = jnp.maximum(i, j), jnp.minimum(i, j)
        source = 128 + ((high * (high - 1)) >> 1) + low
        source = jnp.where((high == low) | (high > 26), -1, source)
        pick = jnp.where(source == iota((128, 512), 1), 1.0, 0.0).astype(BF16)
        square_ref[pl.ds(pl.multiple_of(b * 128, 128), 128), :] = jnp.dot(
            pick, tall[...], preferred_element_type=F32
        ).astype(BF16)

    pass_on(order[2])
    pass_on(order[3])
    for copy in copies:
        copy.wait_recv()
    for copy in staged:
        copy.wait()
    main_kernel(
        place_at, got_ref, near_ref, bottom_ref, top_ref, square_ref, out_weight_ref, click_ref,
        hot_value_ref, low_ref, grad_ref, terms, rows_in, stack, far, pairs, hidden, slope,
    )
    for k in range(16):
        want_flat[k * 8 : k * 8 + 8, :] = want_ref[k]

    along, flat = {}, []

    def set_out(dy):
        @pl.loop(0, 8)
        def _(d):
            for tile in range(13):
                picked = []
                for e in range(16):
                    dx, p = (tile // 3, tile % 3 * 16 + e) if tile < 12 else (e // 4, EARLY + e % 4)
                    picked.append(terms[pl.ds(term_at[d, dy * 4 + dx, p], 1), :])
                leaving[dy, d, tile * 16 : tile * 16 + 16, :] = jnp.concatenate(picked, axis=0).astype(BF16)

        for d in range(1, 8):
            along[dy, d] = send(leaving.at[dy, d], onward.at[dy, d], zs[d - 1])
        onward[dy, 0] = leaving[dy, 0]

    def hand_on(dy):
        for d in range(1, 8):
            along[dy, d].wait_recv()
        for dx in range(4):
            early = onward.at[dy, :, pl.ds(dx * EARLY, EARLY)]
            late = onward.at[dy, :, pl.ds(4 * EARLY, 16)]
            k = dy * 4 + dx
            if k:
                flat.append(send(early, come.at[k, :, pl.ds(0, EARLY)], xys[k - 1]))
                flat.append(send(late, come.at[k, :, pl.ds(EARLY, 16)], xys[k - 1]))
            else:
                come[0, :, 0:EARLY, :] = onward[0, :, 0:EARLY, :]
                come[0, :, EARLY:64, :] = onward[0, :, 4 * EARLY : 4 * EARLY + 16, :]

    set_out(2)
    set_out(1)
    hot_kernel(hot_row_ref, hot_value_ref, bottom_ref, low_ref, grad_ref, in_ref, hot_halves, top)

    mine, other = core * 4096, (1 - core) * 4096
    own = (x, y)
    plan = [(which, d) for d in (1, 2, 3, 0) for which in (0, 1)]
    starts = [which * 2048 + lax.rem(own[which] + d, 4) * 512 for which, d in plan]
    over = [send(in_ref.at[rows_at(other + start, 512)], core_buf.at[rows_at(start, 512)], partner) for start in starts]
    hand_on(2)
    set_out(3)
    first = {}
    for (which, d), start, copy in zip(plan, starts, over):
        copy.wait_recv()
        if d:

            @pl.loop(0, 2)
            def _(step):
                here = rows_at(start + step * 256, 256)
                value = in_ref[rows_at(mine + start + step * 256, 256), :].astype(F32)
                half[here, :] = (value + core_buf[here, :].astype(F32)).astype(BF16)

            first[which, d] = send(
                half.at[rows_at(start, 512)], buf1.at[which, d - 1], (xs, ys)[which][d - 1]
            )
    hand_on(1)
    set_out(0)
    second = {}
    for which in range(2):
        for d in range(1, 4):
            first[which, d].wait_recv()
        for d in (1, 2, 3, 0):
            piece = lax.rem(own[1 - which] + d, 4) * 128
            here = rows_at(piece, 128)
            start = which * 2048 + own[which] * 512 + piece
            total = in_ref[rows_at(mine + start, 128), :].astype(F32) + core_buf[rows_at(start, 128), :].astype(F32)
            for e in range(3):
                total += buf1[which, e, here, :].astype(F32)
            if d:
                sum1[which, here, :] = total.astype(BF16)
                second[which, d] = send(sum1.at[which, here], buf2.at[which, d - 1], (ys, xs)[which][d - 1])
            else:
                sum2[:, which] = total.reshape(8, 16, 128)
    for which in range(2):
        for d in range(1, 4):
            second[which, d].wait_recv()
        sum2[:, which] = sum2[:, which] + (
            buf2[which, 0].astype(F32) + buf2[which, 1].astype(F32) + buf2[which, 2].astype(F32)
        ).reshape(8, 16, 128)
    third = [send(sum2.at[lax.rem(z + d, 8)], buf3.at[d - 1], zs[d - 1]) for d in range(1, 8)]
    hand_on(3)
    for copy in third:
        copy.wait_recv()
    total = sum2[z]
    for d in range(7):
        total += buf3[d]
    base = (mine + x * 512 + y * 128, mine + 2048 + y * 512 + x * 128)
    back = {}
    for which in range(2):
        block = out_ref.at[rows_at(base[which] + z * 16, 16)]
        out_ref[rows_at(base[which] + z * 16, 16), :] = total[which].astype(BF16)
        for d in range(1, 8):
            back[which, d] = send(block, block, zs[d - 1])
    hand_on(0)
    spread = {}
    for which in range(2):
        for d in range(1, 8):
            back[which, d].wait_recv()
        block = out_ref.at[rows_at(base[which], 128)]
        for d in range(1, 4):
            spread[which, d] = send(block, block, (ys, xs)[which][d - 1])
    for copy in flat:
        copy.wait_recv()
    cold_start(want_flat, come, halves, joined)
    last, across = {}, []
    for which in range(2):
        for d in range(1, 4):
            spread[which, d].wait_recv()
        block = out_ref.at[rows_at(mine + which * 2048 + own[which] * 512, 512)]
        for d in range(1, 4):
            last[which, d] = send(block, block, (xs, ys)[which][d - 1])
        across.append(send(block, block, partner))
    for n in range(4):
        cold_step(n, part_ref, halves, joined)
        for low_row in (n * 512, n * 512 + 2048):
            block = pl.ds(low_row, 512)
            across.append(send(part_ref.at[block], other_ref.at[block], partner))
        if n == 2:
            for d in range(1, 4):
                for which in range(2):
                    last[which, d].wait_recv()
                    block = out_ref.at[rows_at(mine + which * 2048 + lax.rem(own[which] + 4 - d, 4) * 512, 512)]
                    across.append(send(block, block, partner))
    for copy in across:
        copy.wait_recv()
    for copy in started:
        copy.wait_send()


def whole(owner, row, table, index, hot_table, dense, weight, top, out_weight, clicks):
    vmem = pl.BlockSpec(memory_space=pltpu.VMEM)
    return pl.pallas_call(
        whole_kernel,
        out_shape=(
            jax.ShapeDtypeStruct((8192, 128), BF16),
            jax.ShapeDtypeStruct((4096, 128), BF16),
            jax.ShapeDtypeStruct((4096, 128), BF16),
        ),
        in_specs=[pl.BlockSpec(memory_space=pl.ANY)] * 8 + [vmem] * 2,
        out_specs=(vmem,) * 3,
        scratch_shapes=[
            pltpu.VMEM((13, 256), jnp.int32),
            pltpu.VMEM((13, 256), jnp.int32),
            pltpu.VMEM((4096, 128), BF16),
            pltpu.VMEM((13, 256), jnp.int32),
            pltpu.VMEM((4096, 128), BF16),
            pltpu.VMEM((256, 256), BF16),
            pltpu.VMEM((256, 128), BF16),
            pltpu.VMEM((479, 1024), BF16),
            pltpu.VMEM((512, 1024), BF16),
            pltpu.VMEM((8, 16, 128), jnp.int32),
            pltpu.VMEM((8, 16, 128), jnp.int32),
            pltpu.VMEM((16, 256), jnp.int32),
            pltpu.VMEM((256, 128), F32),
            pltpu.VMEM((256, 128), F32),
            pltpu.VMEM((128, 128), F32),
            pltpu.VMEM((16, 8, 128), jnp.int32),
            pltpu.VMEM((128, 128), jnp.int32),
            pltpu.VMEM((8, 16, 128), jnp.int32),
            pltpu.VMEM((16, 8, 128), jnp.int32),
            pltpu.VMEM((16, 8, 128), jnp.int32),
            pltpu.VMEM((4096, 128), F32),
            pltpu.VMEM((4096, 128), F32),
            pltpu.VMEM((256, 128), F32),
            pltpu.VMEM((4, 8, 208, 128), BF16),
            pltpu.VMEM((4, 8, 208, 128), BF16),
            pltpu.VMEM((16, 8, 64, 128), BF16),
            pltpu.VMEM((32, 112, 128), BF16),
            pltpu.VMEM((256, 128), BF16),
            pltpu.VMEM((896, 1024), BF16),
            pltpu.VMEM((13, 256, 128), F32),
            pltpu.VMEM((256, 896), BF16),
            pltpu.VMEM((256, 1024), BF16),
            pltpu.VMEM((3336, 128), F32),
            pltpu.VMEM((8192, 128), F32),
            pltpu.VMEM((32, 256, 128), BF16),
            pltpu.VMEM((4, 144, 128), F32),
            pltpu.VMEM((256, 896), F32),
            pltpu.VMEM((256, 1024), F32),
            pltpu.VMEM((256, 1024), F32),
            pltpu.VMEM((8192, 128), BF16),
            pltpu.VMEM((3328, 256), BF16),
            pltpu.VMEM((480, 1024), F32),
            pltpu.VMEM((4, 8, 208, 128), BF16),
            pltpu.VMEM((4, 8, 208, 128), BF16),
            pltpu.VMEM((16, 8, 64, 128), BF16),
            pltpu.VMEM((8192, 256), BF16),
            pltpu.VMEM((64, 128), jnp.int32),
            pltpu.VMEM((4096, 128), BF16),
            pltpu.VMEM((4096, 128), BF16),
            pltpu.VMEM((2, 3, 512, 128), BF16),
            pltpu.VMEM((2, 512, 128), BF16),
            pltpu.VMEM((2, 3, 128, 128), BF16),
            pltpu.VMEM((8, 2, 16, 128), F32),
            pltpu.VMEM((7, 2, 16, 128), F32),
            pltpu.SMEM((13, 256), jnp.int32),
            pltpu.SMEM((16, 8, 128), jnp.int32),
            pltpu.SMEM((8, 16, 128), jnp.int32),
            pltpu.SMEM((16, 256), jnp.int32),
            pltpu.SemaphoreType.DMA((207,)),
            pltpu.SemaphoreType.DMA((207,)),
            pltpu.SemaphoreType.DMA((12,)),
        ],
        compiler_params=pltpu.CompilerParams(collective_id=0, has_side_effects=True, vmem_limit_bytes=VMEM_LIMIT),
        name="whole",
    )(owner, row, table, index, hot_table, dense, weight, top, out_weight, clicks)


def format_kernel(in_ref, part_ref, other_ref, hot_ref, cold_ref, top_ref):
    hot_ref[...] = in_ref[0:4096, :].astype(F32)
    cold_ref[...] = part_ref[...].astype(F32) + other_ref[...].astype(F32)
    for n in range(8):
        top_ref[:, n * 128 : n * 128 + 128] = in_ref[4096 + n * 480 : 4576 + n * 480, :].astype(F32)[0:479, :]


def format_sums(values, part, other):
    return pl.pallas_call(
        format_kernel,
        out_shape=(
            jax.ShapeDtypeStruct((4096, 128), F32),
            jax.ShapeDtypeStruct((4096, 128), F32),
            jax.ShapeDtypeStruct((479, 1024), F32),
        ),
        compiler_params=params(),
        name="format_sums",
    )(values, part, other)


def body(
    dense_feats,
    bottom_weight,
    top_weight,
    out_weight,
    hot_table,
    cold_table,
    hot_index,
    cold_owner,
    cold_row,
    clicks,
):
    sums, part, other = whole(
        cold_owner.T, cold_row.T, cold_table, hot_index.T, hot_table, dense_feats, bottom_weight, top_weight,
        out_weight.reshape(1, 1024), clicks.reshape(1, 256),
    )
    return format_sums(sums, part, other)


def solution(mesh):
    return jax.shard_map(
        body,
        mesh=mesh,
        in_specs=(
            P(("dp", "rep"), None),
            P(),
            P(),
            P(),
            P(),
            P("dp", None),
            P(("dp", "rep"), None),
            P(("dp", "rep"), None),
            P(("dp", "rep"), None),
            P(("dp", "rep")),
        ),
        out_specs=(P(), P("dp", None), P()),
        check_vma=False,
    )
```

time: 532 us -> 170 us (0.32)
  waiting for transfers between devices: 302 us -> 0 us
  Pallas kernels: 0 us -> 167 us
  local copies, waits for them, and re-layouts: 94.7 us -> 1.28 us
  other arithmetic: 70.2 us -> 0 us
  blocking collectives: 26.7 us -> 0 us
  starting transfers between devices: 14.9 us -> 0 us
  between operations: 14.6 us -> 0.64 us
  matrix products: 8.56 us -> 0 us
    psum x2 -> x0, waiting for transfers between devices: 251 us -> none  [the longest x1 214 us: body(): hot_grad = lax.psum(local_hot, ('dp', 'rep'))]
    pallas_call x0 -> x2, Pallas kernels: none -> 167 us  [the longest x1 162 us: whole(): pl.pallas_call(whole_kernel, out_shape=(jax.ShapeDtypeStruct((8192, 128),...]
    scatter-add x2 -> x0, other arithmetic: 59 us -> none  [the longest x1 37.6 us: body(): local_cold = jnp.zeros((cold_table.shape[0], width), jnp.float32).at[want...]
    all_to_all x2 -> x0, waiting for transfers between devices: 51.5 us -> none  [the longest x1 36.9 us: body(): lax.all_to_all(found_rows, 'dp', split_axis=0, concat_axis=0, tiled=True)]
    gather x7 -> x0, local copies, waits for them, and re-layouts: 31.8 us -> none  [the longest x2 13.9 us: body(): found_rows = jnp.take(cold_table, wanted, axis=0)]
    scatter x2 -> x0, local copies, waits for them, and re-layouts: 27.2 us -> none  [the longest x1 14.5 us: body(): jnp.zeros((owners * capacity, width), jnp.bfloat16).at[slot_index]]
    all_to_all x1 -> x0, blocking collectives: 26.7 us -> none  [body(): lax.all_to_all(requests, 'dp', split_axis=0, concat_axis=0, tiled=True)]
    all_to_all x2 -> x0, starting transfers between devices: 14.9 us -> none  [the longest x1 7.59 us: body(): lax.all_to_all(found_rows, 'dp', split_axis=0, concat_axis=0, tiled=True)]
  transfers between devices with their start and end apart: 4 -> 0, of which waited for: 4 -> 0; matrix products, arithmetic and copies ran while one was open for 15% -> 0% of each run, Pallas kernels for 0% -> 0%
where the time goes in v1:
time: 170 us; the launch traced here: 169 us
  Pallas kernels  167 us (98%)
    pallas_call x1, Pallas kernels, whole(): pl.pallas_call(whole_kernel, out_shape=(jax.ShapeDtypeStruct((8192, 128),...  162 us
    pallas_call x1, Pallas kernels, format_sums(): pl.pallas_call(format_kernel, out_shape=(jax.ShapeDtypeStruct((4096, 128)...  5.03 us

profile of v1, /device:TPU:1, one launch (start us, length us, event | category | flops | bytes accessed | tf_op | source)
XLA Modules:
  0.0 168.8 jit_solution(14623522616237638212)
XLA Ops:
  0.6 1.3 reshape.12.out_weight_ref
  1.9 161.8 %whole.1 = (bf16[8192,128]{1,0:T(8,128)(2,1)}, bf16[4096,128]{1,0:T(8,128)(2,1)}, bf16[4096,128]{1,0:T(8,128)(2,1)}) custom-call(s32[13,256]{1,0:T(8,128)} %bitcast.4, s32[13,256]{1,0:T(8,128)} %bitcast.5, bf16[4096,128]{1,0:T(8,128)(2,1)} %table_far.1, s32[13,256]{1,0:T(8,128)} %bitcast.6, bf16[4096,128]{1,0:T(8,128)(2,1)} %hot_table_far.1, ...), custom_call_target="tpu_custom_call" | custom-call | tf_op jit(solution)/shard_map/whole/pallas_call | solution.py:547
  163.7 5.0 %format_sums.1 = (f32[4096,128]{1,0:T(8,128)}, f32[4096,128]{1,0:T(8,128)}, f32[479,1024]{1,0:T(8,128)}) custom-call(bf16[8192,128]{1,0:T(8,128)(2,1)} %get-tuple-element.6.in_ref, bf16[4096,128]{1,0:T(8,128)(2,1)} %get-tuple-element.7.part_ref, bf16[4096,128]{1,0:T(8,128)(2,1)} %get-tuple-element.8.other_ref), custom_call_target="tpu_custom_call" | custom-call | tf_op jit(solution)/shard_map/format_sums/pallas_call | solution.py:632

commit v2 on v1

--- a/solution.py
+++ b/solution.py
@@ -444,7 +444,6 @@
                 come[0, :, EARLY:64, :] = onward[0, :, 4 * EARLY : 4 * EARLY + 16, :]
 
     set_out(2)
-    set_out(1)
     hot_kernel(hot_row_ref, hot_value_ref, bottom_ref, low_ref, grad_ref, in_ref, hot_halves, top)
 
     mine, other = core * 4096, (1 - core) * 4096
@@ -452,8 +451,7 @@
     plan = [(which, d) for d in (1, 2, 3, 0) for which in (0, 1)]
     starts = [which * 2048 + lax.rem(own[which] + d, 4) * 512 for which, d in plan]
     over = [send(in_ref.at[rows_at(other + start, 512)], core_buf.at[rows_at(start, 512)], partner) for start in starts]
-    hand_on(2)
-    set_out(3)
+    set_out(1)
     first = {}
     for (which, d), start, copy in zip(plan, starts, over):
         copy.wait_recv()
@@ -468,8 +466,8 @@
             first[which, d] = send(
                 half.at[rows_at(start, 512)], buf1.at[which, d - 1], (xs, ys)[which][d - 1]
             )
-    hand_on(1)
-    set_out(0)
+    hand_on(2)
+    set_out(3)
     second = {}
     for which in range(2):
         for d in range(1, 4):
@@ -486,6 +484,8 @@
                 second[which, d] = send(sum1.at[which, here], buf2.at[which, d - 1], (ys, xs)[which][d - 1])
             else:
                 sum2[:, which] = total.reshape(8, 16, 128)
+    hand_on(1)
+    set_out(0)
     for which in range(2):
         for d in range(1, 4):
             second[which, d].wait_recv()

time: 170 us -> 167 us (0.982)
  Pallas kernels: 167 us -> 165 us
    pallas_call x1, Pallas kernels: 162 us -> 160 us  [whole(): pl.pallas_call(whole_kernel, out_shape=(jax.ShapeDtypeStruct((8192, 128),...]
where the time goes in v2:
time: 167 us; the launch traced here: 166 us
  Pallas kernels  165 us (99%)
    pallas_call x1, Pallas kernels, whole(): pl.pallas_call(whole_kernel, out_shape=(jax.ShapeDtypeStruct((8192, 128),...  160 us
    pallas_call x1, Pallas kernels, format_sums(): pl.pallas_call(format_kernel, out_shape=(jax.ShapeDtypeStruct((4096, 128)...  5.03 us

profile of v2, /device:TPU:1, one launch (start us, length us, event | category | flops | bytes accessed | tf_op | source)
XLA Modules:
  0.0 166.5 jit_solution(5332991473936227643)
XLA Ops:
  0.6 1.3 reshape.12.out_weight_ref
  1.9 159.5 %whole.1 = (bf16[8192,128]{1,0:T(8,128)(2,1)}, bf16[4096,128]{1,0:T(8,128)(2,1)}, bf16[4096,128]{1,0:T(8,128)(2,1)}) custom-call(s32[13,256]{1,0:T(8,128)} %bitcast.4, s32[13,256]{1,0:T(8,128)} %bitcast.5, bf16[4096,128]{1,0:T(8,128)(2,1)} %table_far.1, s32[13,256]{1,0:T(8,128)} %bitcast.6, bf16[4096,128]{1,0:T(8,128)(2,1)} %hot_table_far.1, ...), custom_call_target="tpu_custom_call" | custom-call | tf_op jit(solution)/shard_map/whole/pallas_call | solution.py:547
  161.5 5.0 %format_sums.1 = (f32[4096,128]{1,0:T(8,128)}, f32[4096,128]{1,0:T(8,128)}, f32[479,1024]{1,0:T(8,128)}) custom-call(bf16[8192,128]{1,0:T(8,128)(2,1)} %get-tuple-element.6.in_ref, bf16[4096,128]{1,0:T(8,128)(2,1)} %get-tuple-element.7.part_ref, bf16[4096,128]{1,0:T(8,128)(2,1)} %get-tuple-element.8.other_ref), custom_call_target="tpu_custom_call" | custom-call | tf_op jit(solution)/shard_map/format_sums/pallas_call | solution.py:632
